TPU v7x, 512 devices: a whole 4x4x16 slice. The times are simulated.
512 devices in a mesh: ep: 64 (over y, z_lo, core), dp: 8 (over z_hi, x).
Axes of the slice: x: 4, y: 4, z: 16 (z_hi: 2, z_lo: 8; z = z_hi * 8 + z_lo), core: 2. Of those that a mesh axis runs over, the one named last changes fastest.
Arguments:
- hidden: bfloat16 [2, 16384, 2048], P(None, ('ep', 'dp')), may hold values from -6 to 6
- norm_gain: bfloat16 [2048], replicated, may hold values from 0.5 to 1.5
- gate_weights: float32 [2, 16384, 8], P(None, ('ep', 'dp')), may hold values from 0.05 to 1
- routes: int32 [2, 16384, 8], P(None, ('ep', 'dp')), may hold values from 0 to 63, as said below
- replica_pick: int32 [2, 16384, 8], P(None, ('ep', 'dp')), may hold values from 0 to 4095
- trainer_experts: int32 [64], replicated, may hold values from 0 to 63, each once
- hot_experts: int32 [3], replicated, may hold values from 0 to 63, as said below
- replica_hot: int32 [64], replicated, may hold values from 0 to 2, as said below
- w_gate: bfloat16 [64, 2048, 384], P('ep', 'dp'), may hold values from -0.125 to 0.125
- w_up: bfloat16 [64, 2048, 384], P('ep', 'dp'), may hold values from -0.125 to 0.125
- w_down: bfloat16 [64, 384, 2048], P('ep', None, 'dp'), may hold values from -0.3125 to 0.3125
- queries: bfloat16 [2, 16384, 4096], P(None, ('ep', 'dp')), may hold values from -6 to 6
- key_cache: bfloat16 [16384, 32, 512], P(('ep', 'dp')), may hold values from -6 to 6
- value_cache: bfloat16 [16384, 32, 512], P(('ep', 'dp')), may hold values from -6 to 6
- new_keys: bfloat16 [2, 16384, 512], P(None, ('ep', 'dp')), may hold values from -6 to 6
- new_values: bfloat16 [2, 16384, 512], P(None, ('ep', 'dp')), may hold values from -6 to 6
- cache_lengths: int32 [16384], P(('ep', 'dp')), may hold values from 2 to 32, as said below
Outputs:
- mixed: bfloat16 [2, 16384, 2048], P(None, ('ep', 'dp'))
- context: bfloat16 [2, 16384, 4096], P(None, ('ep', 'dp'))
Inputs may be any that keep to these rules, and one draw needn't show every extreme that they name: Trainer index p holds expert trainer_experts[p]; each expert once. `hot_experts`: 3 different experts, among them expert 0 and expert 64 - 1. `replica_hot`: every entry of hot_experts is named by some index. `cache_lengths`: the 32 sequences of each device include one with 32 live entries. `routes`: each row names 8 different experts; every expert is named by some row.
All inputs are finite; a program needn't handle non-finite values.
Results may differ from a plain program's by a relative error of at most 0.001.
The roundings to bfloat16 on the way count: a program that leaves them out, or rounds other values in their place, can miss the bound.
Values may be sent and summed in bfloat16 or wider, within the bound.
A program may use at most 64 MiB of HBM per device.

v0:
```python
import math
import jax
import jax.numpy as jnp
from jax import lax
from jax.sharding import PartitionSpec as P

HEADS = 32
KV_HEADS = 4
HEAD = 128
TOP = 8
CAP = 3
SLOTS = 2
norm_epsilon = 1e-06


def spread(shard, axis, root):
    mine = lax.axis_index(axis) == root
    return lax.psum(jnp.where(mine, shard, jnp.zeros_like(shard)), axis)


def scaled_norm(hidden_rows, norm_gain):
    values = hidden_rows.astype(jnp.float32)
    mean_square = jnp.mean(values * values, axis=-1, keepdims=True)
    return (values * lax.rsqrt(mean_square + norm_epsilon) * norm_gain.astype(jnp.float32)).astype(
        jnp.bfloat16
    )


def table_lookup(onehot_rows, table):
    return jnp.dot(onehot_rows, table, preferred_element_type=jnp.int32)


def attend(query_rows, key_cache, value_cache, new_keys, new_values, cache_lengths, step_index):
    rows_here = query_rows.shape[0]
    cache_len = key_cache.shape[1]
    steps_all = new_keys.shape[0]
    grouped = query_rows.reshape(rows_here, KV_HEADS, HEADS // KV_HEADS, HEAD)
    keys_cached = key_cache.reshape(rows_here, cache_len, KV_HEADS, HEAD)
    values_cached = value_cache.reshape(rows_here, cache_len, KV_HEADS, HEAD)
    keys_fresh = new_keys.reshape(steps_all, rows_here, KV_HEADS, HEAD)
    values_fresh = new_values.reshape(steps_all, rows_here, KV_HEADS, HEAD)
    score_scale = 1.0 / math.sqrt(HEAD)
    cache_scores = (
        jnp.einsum("rkgh,rckh->rkgc", grouped, keys_cached, preferred_element_type=jnp.float32)
        * score_scale
    )
    fresh_scores = (
        jnp.einsum("rkgh,srkh->rkgs", grouped, keys_fresh, preferred_element_type=jnp.float32)
        * score_scale
    )
    cache_mask = (jnp.arange(cache_len, dtype=jnp.int32)[None, :] < cache_lengths[:, None])[
        :, None, None, :
    ]
    fresh_mask = (jnp.arange(steps_all, dtype=jnp.int32) <= step_index)[None, None, None, :]
    row_max = jnp.maximum(
        jnp.max(jnp.where(cache_mask, cache_scores, -1e30), axis=-1),
        jnp.max(jnp.where(fresh_mask, fresh_scores, -1e30), axis=-1),
    )
    cache_exp = jnp.where(cache_mask, jnp.exp(cache_scores - row_max[..., None]), 0.0)
    fresh_exp = jnp.where(fresh_mask, jnp.exp(fresh_scores - row_max[..., None]), 0.0)
    row_total = jnp.sum(cache_exp, axis=-1) + jnp.sum(fresh_exp, axis=-1)
    cache_probs = (cache_exp / row_total[..., None]).astype(jnp.bfloat16)
    fresh_probs = (fresh_exp / row_total[..., None]).astype(jnp.bfloat16)
    summed = jnp.einsum(
        "rkgc,rckh->rkgh", cache_probs, values_cached, preferred_element_type=jnp.float32
    )
    summed = summed + jnp.einsum(
        "rkgs,srkh->rkgh", fresh_probs, values_fresh, preferred_element_type=jnp.float32
    )
    return summed.astype(jnp.bfloat16).reshape(rows_here, HEADS * HEAD)


def body(
    hidden,
    norm_gain,
    gate_weights,
    routes,
    replica_pick,
    trainer_experts,
    hot_experts,
    replica_hot,
    w_gate,
    w_up,
    w_down,
    queries,
    key_cache,
    value_cache,
    new_keys,
    new_values,
    cache_lengths,
):
    ep_count = lax.axis_size("ep")
    my_device = lax.axis_index("ep")
    device_ids = jnp.arange(ep_count, dtype=jnp.int32)
    expert_count = trainer_experts.shape[0]
    expert_ids = jnp.arange(expert_count, dtype=jnp.int32)
    hot_count = hot_experts.shape[0]
    hot_ids = jnp.arange(hot_count, dtype=jnp.int32)
    home_device = jnp.sum(
        jnp.where(trainer_experts[None, :] == expert_ids[:, None], device_ids[None, :], 0), axis=1
    )
    hosted = jnp.sum(
        jnp.where(replica_hot[:, None] == hot_ids[None, :], hot_experts[None, :], 0), axis=1
    )
    is_replica = (hosted[None, :] == expert_ids[:, None]).astype(jnp.int32)
    replica_order = jnp.cumsum(is_replica, axis=1) * is_replica
    copies = 1 + jnp.sum(is_replica, axis=1)
    my_hot = jnp.sum(jnp.where(device_ids == my_device, replica_hot, 0))
    own_pair = jnp.concatenate([w_gate, w_up], axis=0)
    replica_pair = jnp.zeros_like(own_pair)
    replica_down = jnp.zeros_like(w_down)
    for hot_index in range(hot_count):
        hot_expert = jnp.sum(jnp.where(hot_ids == hot_index, hot_experts, 0))
        root_device = jnp.sum(jnp.where(expert_ids == hot_expert, home_device, 0))
        sent_pair, sent_down = (
            spread(own_pair, "ep", root_device),
            spread(w_down, "ep", root_device),
        )
        wanted = my_hot == hot_index
        replica_pair = jnp.where(wanted, sent_pair, replica_pair)
        replica_down = jnp.where(wanted, sent_down, replica_down)
    slot_pair, slot_down = (
        lax.all_gather(jnp.stack([own_pair, replica_pair]), "dp", axis=2, tiled=True),
        lax.all_gather(jnp.concatenate([w_down, replica_down], axis=0), "dp", axis=2, tiled=True),
    )
    tokens_here = hidden.shape[1]
    width = hidden.shape[2]
    entries = tokens_here * TOP
    slot_total = ep_count * SLOTS
    buffer_rows = slot_total * CAP
    entry_ids = jnp.arange(entries, dtype=jnp.int32)
    token_map = (
        (entry_ids // TOP)[:, None] == jnp.arange(tokens_here, dtype=jnp.int32)[None, :]
    ).astype(jnp.float32)
    contract_first = (((0,), (0,)), ((), ()))
    mixed_steps = []
    context_steps = []
    for step_index in range(hidden.shape[0]):
        context_steps.append(
            attend(
                queries[step_index],
                key_cache,
                value_cache,
                new_keys,
                new_values,
                cache_lengths,
                step_index,
            )
        )
        normed = scaled_norm(hidden[step_index], norm_gain)
        weights_top = gate_weights[step_index]
        gates = (weights_top / jnp.sum(weights_top, axis=-1, keepdims=True)).astype(jnp.bfloat16)
        chosen = routes[step_index].reshape(entries)
        replica_picks = replica_pick[step_index].reshape(entries)
        expert_onehot = (chosen[:, None] == expert_ids[None, :]).astype(jnp.int32)
        replica_index = replica_picks % table_lookup(expert_onehot, copies)
        order_rows = table_lookup(expert_onehot, replica_order)
        replica_device = jnp.sum(
            jnp.where(order_rows == replica_index[:, None], device_ids[None, :], 0), axis=1
        )
        target = jnp.where(
            replica_index == 0, table_lookup(expert_onehot, home_device), replica_device
        )
        second_slot = (replica_index > 0).astype(jnp.int32)
        slot_index = target * SLOTS + second_slot
        slot_onehot = (
            slot_index[:, None] == jnp.arange(slot_total, dtype=jnp.int32)[None, :]
        ).astype(jnp.int32)
        slot_rank = jnp.sum(jnp.cumsum(slot_onehot, axis=0) * slot_onehot, axis=1) - 1
        is_kept = slot_rank < CAP
        row_index = second_slot * (ep_count * CAP) + target * CAP + slot_rank
        placed = (
            is_kept[:, None]
            & (row_index[:, None] == jnp.arange(buffer_rows, dtype=jnp.int32)[None, :])
        ).astype(jnp.float32)
        dispatch = lax.dot_general(placed, token_map, contract_first).astype(jnp.bfloat16)
        weighted = placed * gates.reshape(entries).astype(jnp.float32)[:, None]
        combine_map = lax.dot_general(token_map, weighted, contract_first).astype(jnp.bfloat16)
        outgoing = jnp.dot(dispatch, normed, preferred_element_type=jnp.float32).astype(
            jnp.bfloat16
        )
        outgoing = outgoing.reshape(SLOTS, ep_count, CAP, width)
        incoming = lax.all_to_all(outgoing, "ep", split_axis=1, concat_axis=1, tiled=True)
        slot_rows = incoming.reshape(SLOTS, ep_count * CAP, width)
        projected = jnp.einsum(
            "snd,skdf->sknf", slot_rows, slot_pair, preferred_element_type=jnp.float32
        )
        hidden_units = (jax.nn.silu(projected[:, 0]) * projected[:, 1]).astype(jnp.bfloat16)
        expert_out = jnp.einsum(
            "snf,sfd->snd", hidden_units, slot_down, preferred_element_type=jnp.float32
        ).astype(jnp.bfloat16)
        expert_out = expert_out.reshape(SLOTS, ep_count, CAP, width)
        returned = lax.all_to_all(
            expert_out, "ep", split_axis=1, concat_axis=1, tiled=True
        ).reshape(buffer_rows, width)
        mixed_rows = hidden[step_index].astype(jnp.float32) + jnp.dot(
            combine_map, returned, preferred_element_type=jnp.float32
        )
        mixed_steps.append(mixed_rows.astype(jnp.bfloat16))
    return (jnp.stack(mixed_steps), jnp.stack(context_steps))


def solution(mesh):
    return jax.shard_map(
        body,
        mesh=mesh,
        in_specs=(
            P(None, ("ep", "dp"), None),
            P(),
            P(None, ("ep", "dp"), None),
            P(None, ("ep", "dp"), None),
            P(None, ("ep", "dp"), None),
            P(),
            P(),
            P(),
            P("ep", "dp", None),
            P("ep", "dp", None),
            P("ep", None, "dp"),
            P(None, ("ep", "dp"), None),
            P(("ep", "dp"), None, None),
            P(("ep", "dp"), None, None),
            P(None, ("ep", "dp"), None),
            P(None, ("ep", "dp"), None),
            P(("ep", "dp")),
        ),
        out_specs=(P(None, ("ep", "dp"), None), P(None, ("ep", "dp"), None)),
        check_vma=False,
    )
```

profile of v0, /device:TPU:1, one launch (start us, length us, event | category | flops | bytes accessed | tf_op | source)
XLA Modules:
  0.0 1533.9 jit_solution(9489303480555903428)
XLA Ops:
  7.2 0.8 select_reduce_fusion.4
  8.1 1.4 fusion.152
  9.5 2.7 fusion.153
  14.0 0.9 constant_dynamic-update-slice_fusion.1
  15.0 1.0 constant_dynamic-update-slice_fusion
  16.0 1.8 broadcast_select_fusion.3
  17.7 1.0 broadcast_select_fusion
  21.1 825.0 %all-reduce.3.cloned.1.call-done = (bf16[1,384,256]{2,1,0:T(8,128)(2,1)}, bf16[1,384,256]{2,1,0:T(8,128)(2,1)}, bf16[1,384,256]{2,1,0:T(8,128)(2,1)}, bf16[2,256...) async-done(((bf16[1,384,256]{2,1,0:T(8,128)(2,1)}, bf16[1,384,256]{2,1,0:T(8,128)(2,1)}, bf16[1,384,256]{2,1,0:T(8,128)(2,1)}, ...) | async-done | bytes 1769488 | tf_op jit(solution)/shard_map/psum | solution.py:18
  846.1 1.1 select_bitcast_fusion
  847.2 1.0 pad_maximum_fusion
  851.0 2.1 convolution_convert_fusion.2
  853.0 4.0 reshape.209
  857.0 3.2 copy.100
  860.2 11.6 all-to-all-start.2
  873.8 2.1 convolution_convert_fusion.3
  875.9 4.0 reshape.204
  879.9 3.2 copy.90
  883.1 93.7 %all-to-all-done.2 = bf16[2,64,3,2048]{3,0,2,1:T(2,128)(2,1)} async-done(((bf16[2,64,3,2048]{3,0,2,1:T(2,128)(2,1)}), bf16[2,64,3,2048]{3,0,2,1:T(2,128)(2,1)}, u32[]{:S(2)}, u32[]{:S(2)}) %all-to-all-start.2) | async-done | bytes 1572896 | tf_op jit(solution)/shard_map/all_to_all | solution.py:183
  976.8 6.8 all-to-all-start
  983.8 1.0 select_select_fusion
  984.8 0.8 pad_maximum_fusion.2
  985.6 128.7 %all-gather.3.cloned.1.call-done = bf16[2,2,2048,384]{3,2,1,0:T(8,128)(2,1)} async-done(((bf16[2,2,256,384]{3,2,1,0:T(8,128)(2,1)}), bf16[2,2,2048,384]{3,2,1,0:T(8,128)(2,1)}) %all-gather.3.cloned.1.call-update) | async-done | bytes 6291472 | tf_op jit(solution)/shard_map/all_gather | solution.py:123
  1114.3 6.1 fusion.13
  1120.5 224.6 %all-gather.5.cloned.1.call-done = bf16[2,384,2048]{2,1,0:T(8,128)(2,1)} async-done(((bf16[2,384,256]{2,1,0:T(8,128)(2,1)}), bf16[2,384,2048]{2,1,0:T(8,128)(2,1)}) %all-gather.5.cloned.1.call-update) | async-done | bytes 3145744 | tf_op jit(solution)/shard_map/all_gather | solution.py:124
  1345.1 3.3 convolution_convert_fusion
  1348.3 2.8 copy.103
  1351.1 1.1 copy-done.3
  1352.3 9.7 all-to-all-start.3
  1362.0 5.2 fusion.10
  1367.1 1.0 convolution_convert_fusion.1
  1368.2 2.8 copy.93
  1370.9 64.5 %all-to-all-done.3 = bf16[2,64,3,2048]{3,0,2,1:T(2,128)(2,1)S(1)} async-done(((bf16[2,64,3,2048]{3,0,2,1:T(2,128)(2,1)}), bf16[2,64,3,2048]{3,0,2,1:T(2,128)(2,1)S(1)}, u32[]{:S(2)}, u32[]{:S(2)}) %all-to-all-start.3) | async-done | bytes 1572896 | tf_op jit(solution)/shard_map/all_to_all | solution.py:193
  1435.5 1.1 copy-done.1
  1436.6 8.6 all-to-all-start.1
  1445.2 0.8 slice_reduce_fusion.1
  1448.2 0.7 div.92
  1449.7 0.7 iota_compare_fusion.23
  1450.9 0.8 select_reduce_fusion.1
  1452.1 1.1 fusion.36
  1456.9 0.8 pad_maximum_fusion.1
  1457.8 2.5 copy.104
  1460.3 2.5 reshape.212
  1462.8 55.9 %all-to-all-done.1 = bf16[2,64,3,2048]{3,0,2,1:T(2,128)(2,1)} async-done(((bf16[2,64,3,2048]{3,0,2,1:T(2,128)(2,1)}), bf16[2,64,3,2048]{3,0,2,1:T(2,128)(2,1)}, u32[]{:S(2)}, u32[]{:S(2)}) %all-to-all-start.1) | async-done | bytes 1572896 | tf_op jit(solution)/shard_map/all_to_all | solution.py:193
  1518.6 2.5 copy.94
  1521.2 2.5 reshape.207
  1523.7 2.2 fusion.4
  1526.0 0.7 fusion.5
  1526.7 0.7 pad_maximum_fusion.3
  (148 shorter events, 13.0 us)
Async XLA Ops:
  7.2 1447.5 %copy-start = (bf16[32,32,512]{2,1,0:T(8,128)(2,1)S(1)}, bf16[32,32,512]{2,1,0:T(8,128)(2,1)}, u32[]{:S(2)}) copy-start(bf16[32,32,512]{2,1,0:T(8,128)(2,1)} %param.30) | copy-start | bytes 3145732
  7.2 838.9 %all-reduce.3.cloned.1.call-start = ((), (), s32[]{:S(2)}) async-start(), calls=%async_computation.6 | async-start | bytes 3538944 | tf_op jit(solution)/shard_map/psum | solution.py:18
  17.7 1.1 copy-start.30
  18.8 1095.6 %all-gather.3.cloned.1.call-start = ((), (), s32[]{:S(2)}) async-start(), calls=%async_computation.4 | async-start | bytes 7077888 | tf_op jit(solution)/shard_map/all_gather | solution.py:123
  847.2 1.1 copy-start.15
  847.2 1.3 copy-start.16
  847.2 1.5 copy-start.26
  847.2 3.3 copy-start.17
  847.2 3.5 copy-start.4
  850.9 6.1 copy-start.22
  860.2 116.5 %all-to-all-start.2 = ((bf16[2,64,3,2048]{3,0,2,1:T(2,128)(2,1)}), bf16[2,64,3,2048]{3,0,2,1:T(2,128)(2,1)}, u32[]{:S(2)}, u32[]{:S(2)}) async-start(bf16[2,64,3,2048]{3,0,2,1:T(2,128)(2,1)} %copy.100), calls=%async_computation.2 | async-start | bytes 3145728 | tf_op jit(solution)/shard_map/all_to_all | solution.py:183
  873.7 6.2 copy-start.24
  883.1 101.7 %copy-start.6 = (bf16[1,384,256]{2,1,0:T(8,128)(2,1)S(1)}, bf16[1,384,256]{2,1,0:T(8,128)(2,1)}, u32[]{:S(2)}) copy-start(bf16[1,384,256]{2,1,0:T(8,128)(2,1)} %param.27) | copy-start | bytes 589828
  976.8 374.4 %all-to-all-start = ((bf16[2,64,3,2048]{3,0,2,1:T(2,128)(2,1)}), bf16[2,64,3,2048]{3,0,2,1:T(2,128)(2,1)S(1)}, u32[]{:S(2)}, u32[]{:S(2)}) async-start(bf16[2,64,3,2048]{3,0,2,1:T(2,128)(2,1)} %copy.90), calls=%async_computation | async-start | bytes 3145728 | tf_op jit(solution)/shard_map/all_to_all | solution.py:183
  983.6 361.5 %all-gather.5.cloned.1.call-start = ((), (), s32[]{:S(2)}) async-start(), calls=%async_computation.5 | async-start | bytes 3538944 | tf_op jit(solution)/shard_map/all_gather | solution.py:124
  1351.1 1.1 copy-start.3
  1352.3 83.2 %all-to-all-start.3 = ((bf16[2,64,3,2048]{3,0,2,1:T(2,128)(2,1)}), bf16[2,64,3,2048]{3,0,2,1:T(2,128)(2,1)S(1)}, u32[]{:S(2)}, u32[]{:S(2)}) async-start(bf16[2,64,3,2048]{3,0,2,1:T(2,128)(2,1)} %bitcast.156), calls=%async_computation.3 | async-start | bytes 3145728 | tf_op jit(solution)/shard_map/all_to_all | solution.py:193
  1362.0 5.2 copy-start.29
  1435.5 1.1 copy-start.1
  1435.5 13.4 copy-start.7
  1436.6 82.0 %all-to-all-start.1 = ((bf16[2,64,3,2048]{3,0,2,1:T(2,128)(2,1)}), bf16[2,64,3,2048]{3,0,2,1:T(2,128)(2,1)}, u32[]{:S(2)}, u32[]{:S(2)}) async-start(bf16[2,64,3,2048]{3,0,2,1:T(2,128)(2,1)} %bitcast.155), calls=%async_computation.1 | async-start | bytes 3145728 | tf_op jit(solution)/shard_map/all_to_all | solution.py:193
  1445.2 3.8 copy-start.11
  1445.2 3.9 copy-start.12
  1448.9 2.0 copy-start.5
  1449.7 3.5 copy-start.27
  1451.6 1.5 copy-start.8
  1452.1 2.1 copy-start.13
  1454.7 0.8 copy-start.10
  1454.7 0.9 copy-start.14
  1454.7 0.9 copy-start.28
  1455.2 1.1 copy-start.9
  1456.2 0.7 copy-start.18
  1456.2 0.7 copy-start.19
  1456.2 0.7 copy-start.20
  1456.2 0.7 copy-start.21
  1521.2 2.5 copy-start.23
  1523.7 2.2 copy-start.2
  1523.7 2.2 copy-start.25
Sparse Core Ops, SparseCore 0:
  18.9 827.1 all-reduce.2
  849.7 264.5 all-gather.2
  1118.4 226.5 all-gather.4
where the time goes:
time: 1540 us; the launch traced here: 1530 us
  waiting for transfers between devices  1390 us (90%)
  local copies, waits for them, and re-layouts  39.7 us (3%)
  starting transfers between devices  37 us (2%)
  matrix products  28.6 us (2%)
  other arithmetic  18.2 us (1%)
  between operations  18 us (1%)
    psum x1, waiting for transfers between devices, spread(): return lax.psum(jnp.where(mine, shard, jnp.zeros_like(shard)), axis)  825 us
    all_gather x1, waiting for transfers between devices, body(): lax.all_gather(jnp.concatenate([w_down, replica_down], axis=0), 'dp', axi...  225 us
    all_gather x1, waiting for transfers between devices, body(): lax.all_gather(jnp.stack([own_pair, replica_pair]), 'dp', axis=2, tiled=T...  129 us
    all_to_all x2, waiting for transfers between devices, body(): lax.all_to_all(expert_out, 'ep', split_axis=1, concat_axis=1, tiled=True)  120 us
    all_to_all x2, waiting for transfers between devices, body(): lax.all_to_all(outgoing, 'ep', split_axis=1, concat_axis=1, tiled=True)  93.7 us
  transfers between devices with their start and end apart: 7, of which 6 were waited for; matrix products, arithmetic and copies ran while one was open for 4% of the time, Pallas kernels for 0%

commit v1 on v0

--- a/solution.py
+++ b/solution.py
@@ -180,7 +180,15 @@
             jnp.bfloat16
         )
         outgoing = outgoing.reshape(SLOTS, ep_count, CAP, width)
-        incoming = lax.all_to_all(outgoing, "ep", split_axis=1, concat_axis=1, tiled=True)
+        incoming = jnp.concatenate(
+            lax.all_to_all(
+                jnp.stack(jnp.split(outgoing, lax.axis_size("ep"), axis=1)),
+                axis_name="ep",
+                split_axis=0,
+                concat_axis=0,
+            ),
+            axis=1,
+        )
         slot_rows = incoming.reshape(SLOTS, ep_count * CAP, width)
         projected = jnp.einsum(
             "snd,skdf->sknf", slot_rows, slot_pair, preferred_element_type=jnp.float32

time: 1540 us -> 1490 us (0.968)
  waiting for transfers between devices: 1390 us -> 1300 us
  local copies, waits for them, and re-layouts: 39.7 us -> 79.3 us
    all_gather x1, waiting for transfers between devices: 129 us -> 246 us  [body(): lax.all_gather(jnp.stack([own_pair, replica_pair]), 'dp', axis=2, tiled=T...]
    all_to_all x2, waiting for transfers between devices: 93.7 us -> 0.01 us  [body(): lax.all_to_all(jnp.stack(jnp.split(outgoing, lax.axis_size('ep'), axis=1)...]
    all_gather x1, waiting for transfers between devices: 225 us -> 143 us  [body(): lax.all_gather(jnp.concatenate([w_down, replica_down], axis=0), 'dp', axi...]
    psum x1, waiting for transfers between devices: 825 us -> 785 us  [spread(): return lax.psum(jnp.where(mine, shard, jnp.zeros_like(shard)), axis)]
    unnamed x68 -> x208, local copies, waits for them, and re-layouts: 4.01 us -> 41.9 us
  transfers between devices with their start and end apart: 7 -> 7, of which waited for: 6 -> 5; matrix products, arithmetic and copies ran while one was open for 4% -> 6% of each run, Pallas kernels for 0% -> 0%
where the time goes in v1:
time: 1490 us
  waiting for transfers between devices  1300 us (87%)
  local copies, waits for them, and re-layouts  79.3 us (5%)
  starting transfers between devices  47.8 us (3%)
  matrix products  30.5 us (2%)
  between operations  18.9 us (1%)
  other arithmetic  17.8 us (1%)
    psum x1, waiting for transfers between devices, spread(): return lax.psum(jnp.where(mine, shard, jnp.zeros_like(shard)), axis)  785 us
    all_gather x1, waiting for transfers between devices, body(): lax.all_gather(jnp.stack([own_pair, replica_pair]), 'dp', axis=2, tiled=T...  246 us
    all_gather x1, waiting for transfers between devices, body(): lax.all_gather(jnp.concatenate([w_down, replica_down], axis=0), 'dp', axi...  143 us
    all_to_all x2, waiting for transfers between devices, body(): lax.all_to_all(expert_out, 'ep', split_axis=1, concat_axis=1, tiled=True)  123 us
    unnamed x208, local copies, waits for them, and re-layouts  41.9 us
  transfers between devices with their start and end apart: 7, of which 5 were waited for; matrix products, arithmetic and copies ran while one was open for 6% of the time, Pallas kernels for 0%

profile of v1, /device:TPU:1, one launch (start us, length us, event | category | flops | bytes accessed | tf_op | source)
XLA Modules:
  0.0 1491.8 jit_solution(10073631238668534866)
XLA Ops:
  7.2 0.8 select_reduce_fusion.5
  8.2 1.3 fusion.178
  9.6 0.7 fusion.179
  10.5 0.8 select_reduce_fusion.4
  13.4 1.1 fusion.56
  14.5 0.7 convert_element_type.141
  15.8 3.0 convolution_convert_fusion.3
  18.8 4.0 reshape.204
  24.4 3.2 copy.533
  27.6 17.5 %all-to-all-start = ((bf16[64,2,1,3,2048]{4,1,3,2,0:T(2,128)(2,1)}), bf16[64,2,1,3,2048]{4,1,3,2,0:T(2,128)(2,1)}, u32[]{:S(2)}, u32[]{:S(2)}) async-start(bf16[64,2,1,3,2048]{4,1,3,2,0:T(2,128)(2,1)} %copy.533), calls=%async_computation | async-start | bytes 3145728 | tf_op jit(solution)/shard_map/all_to_all | solution.py:184
  45.2 0.7 fusion.152
  45.9 2.6 fusion.153
  50.7 1.0 broadcast_select_fusion
  51.8 0.8 broadcast_select_fusion.3
  52.9 0.7 fusion.147
  57.7 2.1 convolution_convert_fusion.2
  59.7 4.0 reshape.209
  88.3 785.4 %all-reduce.3.cloned.1.call-done = (bf16[1,384,256]{2,1,0:T(8,128)(2,1)}, bf16[1,384,256]{2,1,0:T(8,128)(2,1)}, bf16[1,384,256]{2,1,0:T(8,128)(2,1)}, bf16[2,256...) async-done(((bf16[1,384,256]{2,1,0:T(8,128)(2,1)}, bf16[1,384,256]{2,1,0:T(8,128)(2,1)}, bf16[1,384,256]{2,1,0:T(8,128)(2,1)}, ...) | async-done | bytes 1769488 | tf_op jit(solution)/shard_map/psum | solution.py:18
  873.7 1.1 select_bitcast_fusion
  874.8 1.0 pad_maximum_fusion
  890.6 4.9 copy.606
  895.4 11.5 all-to-all-start.2
  907.1 0.8 pad_maximum_fusion.2
  907.9 245.7 %all-gather.3.cloned.1.call-done = bf16[2,2,2048,384]{3,2,1,0:T(8,128)(2,1)} async-done(((bf16[2,2,256,384]{3,2,1,0:T(8,128)(2,1)}), bf16[2,2,2048,384]{3,2,1,0:T(8,128)(2,1)}) %all-gather.3.cloned.1.call-update) | async-done | bytes 6291472 | tf_op jit(solution)/shard_map/all_gather | solution.py:123
  1153.6 6.0 fusion.10
  1159.7 143.0 %all-gather.5.cloned.1.call-done = bf16[2,384,2048]{2,1,0:T(8,128)(2,1)} async-done(((bf16[2,384,256]{2,1,0:T(8,128)(2,1)}), bf16[2,384,2048]{2,1,0:T(8,128)(2,1)}) %all-gather.5.cloned.1.call-update) | async-done | bytes 3145744 | tf_op jit(solution)/shard_map/all_gather | solution.py:124
  1302.7 3.3 convolution_convert_fusion.1
  1305.9 2.8 copy.536
  1308.7 1.1 copy-done.4
  1309.8 9.7 all-to-all-start.1
  1319.6 5.1 fusion.13
  1324.7 1.0 convolution_convert_fusion
  1325.7 2.8 copy.609
  1328.5 64.5 %all-to-all-done.1 = bf16[2,64,3,2048]{3,0,2,1:T(2,128)(2,1)S(1)} async-done(((bf16[2,64,3,2048]{3,0,2,1:T(2,128)(2,1)}), bf16[2,64,3,2048]{3,0,2,1:T(2,128)(2,1)S(1)}, u32[]{:S(2)}, u32[]{:S(2)}) %all-to-all-start.1) | async-done | bytes 1572896 | tf_op jit(solution)/shard_map/all_to_all | solution.py:201
  1393.0 8.7 all-to-all-start.3
  1402.8 0.7 div.97
  1403.9 0.8 iota_compare_fusion.23
  1405.1 0.8 select_reduce_fusion.1
  1406.3 0.8 fusion.36
  1410.4 0.8 pad_maximum_fusion.1
  1411.2 2.5 copy.537
  1413.7 2.5 reshape.207
  1416.3 58.9 %all-to-all-done.3 = bf16[2,64,3,2048]{3,0,2,1:T(2,128)(2,1)} async-done(((bf16[2,64,3,2048]{3,0,2,1:T(2,128)(2,1)}), bf16[2,64,3,2048]{3,0,2,1:T(2,128)(2,1)}, u32[]{:S(2)}, u32[]{:S(2)}) %all-to-all-start.3) | async-done | bytes 1572896 | tf_op jit(solution)/shard_map/all_to_all | solution.py:201
  1475.2 2.5 copy.610
  1477.8 2.5 reshape.212
  1480.3 2.1 fusion.5
  1482.4 2.1 fusion.4
  1484.6 0.7 pad_maximum_fusion.3
  (290 shorter events, 51.6 us)
Async XLA Ops:
  7.2 1401.4 %copy-start = (bf16[32,32,512]{2,1,0:T(8,128)(2,1)S(1)}, bf16[32,32,512]{2,1,0:T(8,128)(2,1)}, u32[]{:S(2)}) copy-start(bf16[32,32,512]{2,1,0:T(8,128)(2,1)} %param.30) | copy-start | bytes 3145732
  8.0 4.5 copy-start.29
  8.1 3.6 copy-start.36
  11.3 34.7 %copy-start.31 = (s32[64]{0:T(128)}, s32[64]{0:T(128)S(1)}, u32[]{:S(2)}) copy-start(s32[64]{0:T(128)S(1)} %select_reduce_fusion.4) | copy-start | bytes 772
  12.1 0.6 copy-start.16
  13.4 2.4 copy-start.19
  13.4 2.4 copy-start.25
  27.6 17.6 %copy-start.33 = (s32[3]{0:T(128)S(1)}, s32[3]{0:T(128)}, u32[]{:S(2)}) copy-start(s32[3]{0:T(128)} %param.23) | copy-start | bytes 40
  27.6 22.9 %copy-start.9 = (bf16[1,256,384]{2,1,0:T(8,128)(2,1)S(1)}, bf16[1,256,384]{2,1,0:T(8,128)(2,1)}, u32[]{:S(2)}) copy-start(bf16[1,256,384]{2,1,0:T(8,128)(2,1)} %param.25) | copy-start | bytes 589828
  27.6 23.0 %copy-start.10 = (bf16[1,256,384]{2,1,0:T(8,128)(2,1)S(1)}, bf16[1,256,384]{2,1,0:T(8,128)(2,1)}, u32[]{:S(2)}) copy-start(bf16[1,256,384]{2,1,0:T(8,128)(2,1)} %param.26) | copy-start | bytes 589828
  27.6 24.1 %copy-start.6 = (bf16[1,384,256]{2,1,0:T(8,128)(2,1)S(1)}, bf16[1,384,256]{2,1,0:T(8,128)(2,1)}, u32[]{:S(2)}) copy-start(bf16[1,384,256]{2,1,0:T(8,128)(2,1)} %param.27) | copy-start | bytes 589828
  27.6 867.8 %all-to-all-start = ((bf16[64,2,1,3,2048]{4,1,3,2,0:T(2,128)(2,1)}), bf16[64,2,1,3,2048]{4,1,3,2,0:T(2,128)(2,1)}, u32[]{:S(2)}, u32[]{:S(2)}) async-start(bf16[64,2,1,3,2048]{4,1,3,2,0:T(2,128)(2,1)} %copy.533), calls=%async_computation | async-start | bytes 3145728 | tf_op jit(solution)/shard_map/all_to_all | solution.py:184
  45.2 828.6 %all-reduce.3.cloned.1.call-start = ((), (), s32[]{:S(2)}) async-start(), calls=%async_computation.6 | async-start | bytes 3538944 | tf_op jit(solution)/shard_map/psum | solution.py:18
  50.7 2.2 copy-start.35
  50.7 2.9 copy-start.18
  50.7 3.1 copy-start.37
  50.7 3.3 copy-start.32
  50.7 3.9 copy-start.17
  50.7 3.9 copy-start.30
  51.8 5.9 copy-start.2
  51.8 5.9 copy-start.24
  52.6 1101.0 %all-gather.3.cloned.1.call-start = ((), (), s32[]{:S(2)}) async-start(), calls=%async_computation.4 | async-start | bytes 7077888 | tf_op jit(solution)/shard_map/all_gather | solution.py:123
  55.6 2.1 copy-start.27
  895.4 11.6 copy-start.11
  895.4 11.6 copy-start.12
  895.4 11.6 copy-start.13
  895.4 11.7 copy-start.7
  895.4 413.3 %all-to-all-start.2 = ((bf16[64,2,1,3,2048]{4,1,3,2,0:T(2,128)(2,1)}), bf16[64,2,1,3,2048]{4,1,3,2,0:T(2,128)(2,1)S(1)}, u32[]{:S(2)}, u32[]{:S(2)}) async-start(bf16[64,2,1,3,2048]{4,1,3,2,0:T(2,128)(2,1)} %copy.606), calls=%async_computation.2 | async-start | bytes 3145728 | tf_op jit(solution)/shard_map/all_to_all | solution.py:184
  907.0 395.7 %all-gather.5.cloned.1.call-start = ((), (), s32[]{:S(2)}) async-start(), calls=%async_computation.5 | async-start | bytes 3538944 | tf_op jit(solution)/shard_map/all_gather | solution.py:124
  1308.7 1.1 copy-start.4
  1309.8 83.2 %all-to-all-start.1 = ((bf16[2,64,3,2048]{3,0,2,1:T(2,128)(2,1)}), bf16[2,64,3,2048]{3,0,2,1:T(2,128)(2,1)S(1)}, u32[]{:S(2)}, u32[]{:S(2)}) async-start(bf16[2,64,3,2048]{3,0,2,1:T(2,128)(2,1)} %bitcast.924), calls=%async_computation.1 | async-start | bytes 3145728 | tf_op jit(solution)/shard_map/all_to_all | solution.py:201
  1319.5 5.2 copy-start.34
  1328.5 73.3 %copy-start.21 = (f32[2,32,8]{1,2,0:T(8,128)S(1)}, f32[2,32,8]{1,2,0:T(8,128)}, u32[]{:S(2)}) copy-start(f32[2,32,8]{1,2,0:T(8,128)} %param.19) | copy-start | bytes 6148
  1328.5 75.1 %copy-start.8 = (bf16[2,32,4096]{2,1,0:T(8,128)(2,1)S(1)}, bf16[2,32,4096]{2,1,0:T(8,128)(2,1)}, u32[]{:S(2)}) copy-start(bf16[2,32,4096]{2,1,0:T(8,128)(2,1)} %param.28) | copy-start | bytes 1572868
  1393.0 10.6 copy-start.1
  1393.0 10.7 copy-start.14
  1393.0 10.8 copy-start.15
  1393.0 82.2 %all-to-all-start.3 = ((bf16[2,64,3,2048]{3,0,2,1:T(2,128)(2,1)}), bf16[2,64,3,2048]{3,0,2,1:T(2,128)(2,1)}, u32[]{:S(2)}, u32[]{:S(2)}) async-start(bf16[2,64,3,2048]{3,0,2,1:T(2,128)(2,1)} %bitcast.923), calls=%async_computation.3 | async-start | bytes 3145728 | tf_op jit(solution)/shard_map/all_to_all | solution.py:201
  1403.7 1.4 copy-start.5
  1409.7 0.7 copy-start.22
  1409.7 0.7 copy-start.23
  1477.7 2.6 copy-start.3
  1477.7 2.6 copy-start.20
  1477.8 2.6 copy-start.26
  1477.8 4.7 copy-start.28
Sparse Core Ops, SparseCore 0:
  52.7 820.9 all-reduce.2
  877.3 276.2 all-gather.2
  1157.7 144.8 all-gather.4
